TPU v7x, 32 devices: a whole 2x2x4 slice. The times are simulated.
32 devices in a mesh: scene: 2 (over x), az: 8 (over z, y), rg: 2 (over core).
Axes of the slice: x: 2, y: 2, z: 4, core: 2. Of those that a mesh axis runs over, the one named last changes fastest.
Arguments:
- complex_phase_image: float32 [2, 1024, 1024], P(None, ('scene', 'az'), 'rg'), parts along dimension 1, may hold values from -6 to 6
- phase_to_topography_factor: float32 [1024, 1024], P(('scene', 'az'), 'rg'), parts along dimension 0, may hold values from 0.5 to 3
- terrain_model_heights: float32 [128, 16, 1024], P(('scene', 'az'), 'rg'), parts along dimension 0, may hold values from -6 to 6
- radar_parcel_listing: int32 [32, 9], P(('scene', 'az', 'rg')), parts along dimension 0, may hold values from -1 to 1023, as said below
- pixel_terrain_position: int32 [1024, 1024], P(('scene', 'az'), 'rg'), parts along dimension 0, may hold values from 0 to 9215, as said below
- multilook_receiving_patch: int32 [65536, 1], P(('scene', 'az', 'rg')), parts along dimension 0, may hold values from 0 to 15; in each aligned block of 2048 rows (0 to 2047, 2048 to 4095, ...) at most 256 rows name the same one
- multilook_base_point: int32 [65536], P(('scene', 'az', 'rg')), parts along dimension 0, may hold values from 0 to 2047
- multilook_splat_shares: float32 [4, 65536], P(None, ('scene', 'az', 'rg')), parts along dimension 1, may hold values from 0 to 1
Outputs:
- geocoded: float32 [2, 256, 256], P(None, ('scene', 'az'), 'rg'), parts along dimension 1
There are 2 independent parts, one for each index of `scene`. A program takes and returns all parts, laid end to end along the dimension named above; each array names one. Nothing has to cross between parts.
Inputs may be any that keep to these rules, and one draw needn't show every extreme that they name: `radar_parcel_listing`: entries are sub-block numbers lat * 16 + lon; each tile lists a rectangle of at most 3 x 3 sub-blocks in row-major order, then -1 padding. Tile (a, r) lists only sub-blocks with c * 8 - 1 <= lat <= (c + 1) * 8 for one map latitude row c (any row, not tied to a) and r * 8 - 1 <= lon <= (r + 1) * 8. Some tile has exactly 9 listed blocks. pixel_terrain_position // 1024 is a listed, non-padding slot of the pixel's own tile. `multilook_receiving_patch`: among the rows of one device (aligned blocks of 2048 rows) at most 256 name one map tile; some map tile is named by exactly 256 rows of some device.
All inputs are finite; a program needn't handle non-finite values.
Results may differ from a plain program's by a relative error of at most 0.00015.
Values sent between devices are 32-bit elements; how exact they have to be, the bound alone decides.
A program may use at most 64 MiB of HBM per device.

v0:
```python
import math

import jax
import jax.numpy as jnp
from jax import lax
from jax.sharding import PartitionSpec as P

PATCH = 64
LOOK = 4


EPS = 1e-06
HIGH = lax.Precision.HIGHEST


def padded_2(value, sides, width):
    for axis, dim in sides:
        size, length = (lax.axis_size(axis), value.shape[dim])
        up = [(i, (i + 1) % size) for i in range(size - 1)]
        down = [(j, i) for i, j in up]
        last = lax.slice_in_dim(value, length - width, length, axis=dim)
        first = lax.slice_in_dim(value, 0, width, axis=dim)
        before = lax.ppermute(last, axis, up)
        after = lax.ppermute(first, axis, down)
        value = jnp.concatenate([before, value, after], axis=dim)
    return value


def passed_along(value, axis, steps):
    count = lax.axis_size(axis)
    first, last = (max(0, -steps), min(count, count - steps))
    return lax.ppermute(value, axis, [(source, source + steps) for source in range(first, last)])


def box_mean(magnitude):
    summed = jnp.zeros_like(magnitude)
    for shift_a in (-1, 0, 1):
        for shift_b in (-1, 0, 1):
            summed = summed + jnp.roll(jnp.roll(magnitude, shift_a, axis=1), shift_b, axis=2)
    return summed / 9.0


def dft_tables():
    steps_idx = jnp.arange(PATCH, dtype=jnp.int32)
    product = steps_idx[:, None] * steps_idx[None, :] % PATCH
    angle_table = product.astype(jnp.float32) * (2.0 * math.pi / PATCH)
    return (jnp.cos(angle_table), jnp.sin(angle_table))


def goldstein(patches):
    cosine_table, sine_table = dft_tables()
    forward = jnp.block([[cosine_table, -sine_table], [sine_table, cosine_table]])
    inverse = jnp.block([[cosine_table, sine_table], [-sine_table, cosine_table]])
    columns = jnp.einsum("phw,wk->phk", patches, forward, precision=HIGH)
    left_cos = jnp.einsum("kh,phc->pkc", cosine_table, columns, precision=HIGH)
    left_sin = jnp.einsum("kh,phc->pkc", sine_table, columns, precision=HIGH)
    spec_re = left_cos[..., :PATCH] + left_sin[..., PATCH:]
    spec_im = left_cos[..., PATCH:] - left_sin[..., :PATCH]
    smooth = box_mean(jnp.sqrt(spec_re * spec_re + spec_im * spec_im))
    spectral_gain = jnp.sqrt(smooth / (jnp.mean(smooth, axis=(1, 2), keepdims=True) + EPS))
    weighted = jnp.concatenate([spec_re * spectral_gain, spec_im * spectral_gain], axis=-1)
    back_cos = jnp.einsum("kh,phc->pkc", cosine_table, weighted, precision=HIGH)
    back_sin = jnp.einsum("kh,phc->pkc", sine_table, weighted, precision=HIGH)
    rows_re = back_cos[..., :PATCH] - back_sin[..., PATCH:]
    rows_im = back_cos[..., PATCH:] + back_sin[..., :PATCH]
    restored = jnp.concatenate([rows_re, rows_im], axis=-1)
    return jnp.einsum("phw,wk->phk", restored, inverse, precision=HIGH) / float(PATCH * PATCH)


def block_coords(block_lists, nlon_count):
    clipped = jnp.maximum(block_lists, 0)
    return (clipped // nlon_count, clipped % nlon_count)


def entry_rank(owner_key, is_valid):
    slots = owner_key.shape[-1]
    same_owner = (owner_key[:, :, None] == owner_key[:, None, :]) & is_valid[:, None, :]
    slot_ids = jnp.arange(slots, dtype=jnp.int32)
    earlier = slot_ids[None, :] < slot_ids[:, None]
    return jnp.sum((same_owner & earlier[None]).astype(jnp.int32), axis=2)


def pack_blocks(block_lists, owner_key, local_block, source_rows, self_key):
    slots = block_lists.shape[-1]
    is_valid = block_lists >= 0
    rank_within = entry_rank(owner_key, is_valid)
    slot_ids = jnp.arange(slots, dtype=jnp.int32)
    matches = (is_valid & (owner_key == self_key))[:, :, None] & (
        rank_within[:, :, None] == slot_ids[None, None, :]
    )
    picked = jnp.sum(jnp.where(matches, local_block[:, :, None], 0), axis=1)
    present = jnp.any(matches, axis=1)
    return jnp.where(present[..., None], source_rows[picked], 0.0)


def unpack_blocks(own_list, owner_key, received):
    slots = own_list.shape[-1]
    is_valid = own_list >= 0
    rank_within = entry_rank(owner_key[None], is_valid[None])[0]
    position = jnp.where(is_valid, owner_key * slots + rank_within, 0)
    return received.reshape(-1, received.shape[-1])[position]


def lookup_heights(height_lookup_table, positions, samples):
    lane_width = min(128, samples)
    table_rows = height_lookup_table.reshape(-1, lane_width)
    row_count = table_rows.shape[0]
    lines, width = positions.shape
    row_ids = jnp.arange(row_count, dtype=jnp.int32)
    lane_ids = jnp.arange(lane_width, dtype=jnp.int32)

    def lookup_block(block_positions):
        flat_positions = block_positions.reshape(-1)
        selector = (flat_positions[:, None] // lane_width == row_ids[None, :]).astype(jnp.float32)
        picked_rows = jnp.dot(
            selector, table_rows, precision=HIGH, preferred_element_type=jnp.float32
        )
        lane_match = (flat_positions % lane_width)[:, None] == lane_ids[None, :]
        return jnp.sum(jnp.where(lane_match, picked_rows, 0.0), axis=1).reshape(
            block_positions.shape
        )

    blocked = positions.reshape(lines // 8, 8, width)
    return lax.map(lookup_block, blocked).reshape(lines, width)


def body(
    complex_phase_image,
    phase_to_topography_factor,
    terrain_model_heights,
    radar_parcel_listing,
    pixel_terrain_position,
    multilook_receiving_patch,
    multilook_base_point,
    multilook_splat_shares,
):
    count_az = lax.axis_size("az")
    count_rg = lax.axis_size("rg")
    tiles = count_az * count_rg
    self_az = lax.axis_index("az")
    self_rg = lax.axis_index("rg")
    parcel_north_coordinate, parcel_east_coordinate, number_terrain_points = (
        terrain_model_heights.shape
    )
    nlon_count = parcel_east_coordinate * count_rg
    own_list = radar_parcel_listing[0]
    lat_own, lon_own = block_coords(own_list, nlon_count)
    all_lists = lax.all_gather(radar_parcel_listing, ("az", "rg"), axis=0, tiled=True)
    lat_all, lon_all = block_coords(all_lists, nlon_count)
    key_all = lat_all // parcel_north_coordinate * count_rg + lon_all // parcel_east_coordinate
    local_all = (lat_all - self_az * parcel_north_coordinate) * parcel_east_coordinate + (
        lon_all - self_rg * parcel_east_coordinate
    )
    outgoing = pack_blocks(
        all_lists,
        key_all,
        local_all,
        terrain_model_heights.reshape(
            parcel_north_coordinate * parcel_east_coordinate, number_terrain_points
        ),
        self_az * count_rg + self_rg,
    )
    received = lax.all_to_all(outgoing, ("az", "rg"), split_axis=0, concat_axis=0, tiled=True)
    key_own = lat_own // parcel_north_coordinate * count_rg + lon_own // parcel_east_coordinate
    height_lookup_table = unpack_blocks(own_list, key_own, received)
    height_values = lookup_heights(
        height_lookup_table, pixel_terrain_position, number_terrain_points
    )
    topo_phase = phase_to_topography_factor * height_values
    cosine_phase = jnp.cos(topo_phase)
    sine_phase = jnp.sin(topo_phase)
    real_part = complex_phase_image[0] * cosine_phase + complex_phase_image[1] * sine_phase
    imag_part = complex_phase_image[1] * cosine_phase - complex_phase_image[0] * sine_phase
    flattened = jnp.stack([real_part, imag_part])
    rim = PATCH // 4
    step = PATCH // 2
    az_lines, rg_samples = phase_to_topography_factor.shape
    padded = padded_2(flattened, (("az", 1), ("rg", 2)), rim)
    block_rows = az_lines // step
    block_cols = rg_samples // step
    row_pieces = padded.reshape(2, block_rows + 1, step, rg_samples + 2 * rim)
    strips = jnp.concatenate([row_pieces[:, :-1], row_pieces[:, 1:]], axis=2)
    col_pieces = strips.reshape(2, block_rows, PATCH, block_cols + 1, step)
    paired = jnp.concatenate([col_pieces[..., :-1, :], col_pieces[..., 1:, :]], axis=-1)
    patches = paired.transpose(1, 3, 2, 0, 4).reshape(block_rows * block_cols, PATCH, 2 * PATCH)
    restored = goldstein(patches).reshape(block_rows, block_cols, PATCH, 2, PATCH)
    core_cells = restored[:, :, rim : rim + step, :, rim : rim + step]
    filtered = core_cells.transpose(3, 0, 2, 1, 4).reshape(2, az_lines, rg_samples)
    map_lat = az_lines // LOOK
    map_lon = rg_samples // LOOK
    look_values = (
        filtered.reshape(2, map_lat, LOOK, map_lon, LOOK)
        .mean(axis=(2, 4))
        .reshape(2, map_lat * map_lon)
    )
    look_total = map_lat * map_lon
    capacity = 2 * look_total // tiles
    owner_tile = multilook_receiving_patch[:, 0]
    tile_ids = jnp.arange(tiles, dtype=jnp.int32)
    counts = jnp.sum((owner_tile[:, None] == tile_ids[None, :]).astype(jnp.int32), axis=0)
    starts = jnp.cumsum(counts) - counts
    sort_order = jnp.argsort(owner_tile, stable=True)
    sorted_owner = owner_tile[sort_order]
    rank_sorted = jnp.arange(look_total, dtype=jnp.int32) - starts[sorted_owner]
    slot_index = (
        jnp.zeros((look_total,), jnp.int32)
        .at[sort_order]
        .set(sorted_owner * capacity + rank_sorted)
    )
    payload = jnp.concatenate([look_values, multilook_splat_shares], axis=0)
    payload_buffer = jnp.zeros((6, tiles * capacity), jnp.float32).at[:, slot_index].set(payload)
    cell_buffer = jnp.zeros((tiles * capacity,), jnp.int32).at[slot_index].set(multilook_base_point)
    got_values, got_cells = (
        lax.all_to_all(
            payload_buffer.reshape(6, tiles, capacity),
            ("az", "rg"),
            split_axis=1,
            concat_axis=1,
            tiled=True,
        ),
        lax.all_to_all(
            cell_buffer.reshape(1, tiles, capacity),
            ("az", "rg"),
            split_axis=1,
            concat_axis=1,
            tiled=True,
        ),
    )
    got_values = got_values.reshape(6, tiles * capacity)
    got_cells = got_cells.reshape(tiles * capacity)
    stride = map_lon + 1
    base = got_cells // map_lon * stride + got_cells % map_lon
    corners = jnp.concatenate([base, base + 1, base + stride, base + stride + 1])
    weights = got_values[2:].reshape(-1)
    contributions = jnp.stack(
        [jnp.tile(got_values[0], 4) * weights, jnp.tile(got_values[1], 4) * weights, weights]
    )
    extended = jnp.zeros((3, (map_lat + 1) * stride), jnp.float32).at[:, corners].add(contributions)
    extended = extended.reshape(3, map_lat + 1, stride)
    carried_col = passed_along(extended[:, :, map_lon], "rg", 1)
    extended = extended.at[:, :, 0].add(carried_col)
    carried_row = passed_along(extended[:, map_lat, :map_lon], "az", 1)
    extended = extended.at[:, 0, :map_lon].add(carried_row)
    main_cells = extended[:, :map_lat, :map_lon]
    return main_cells[:2] / jnp.maximum(main_cells[2:3], 1.0)


def solution(mesh):
    return jax.shard_map(
        body,
        mesh=mesh,
        in_specs=(
            P(None, ("scene", "az"), "rg"),
            P(("scene", "az"), "rg"),
            P(("scene", "az"), "rg", None),
            P(("scene", "az", "rg"), None),
            P(("scene", "az"), "rg"),
            P(("scene", "az", "rg"), None),
            P(("scene", "az", "rg")),
            P(None, ("scene", "az", "rg")),
        ),
        out_specs=P(None, ("scene", "az"), "rg"),
        check_vma=False,
    )
```

profile of v0, /device:TPU:0, one launch (start us, length us, event | category | flops | bytes accessed | tf_op | source)
XLA Modules:
  0.0 290.8 jit_solution(13959791806732536806)
XLA Ops:
  0.0 23.3 %all-gather = s32[16,1,9]{2,1,0:T(1,128)S(1)} all-gather(s32[1,1,9]{2,1,0:T(1,128)} %bitcast.272), channel_id=1, replica_groups=mesh['scene'=2,'az'=8,'rg'=2] {'az','rg'}, dimensions={0}, use_global_device_ids=true | all-gather | bytes 612 | tf_op jit(solution)/shard_map/all_gather | solution.py:148
  26.4 3.7 %all-to-all-start.1 = ((f32[16,9,1024]{2,1,0:T(8,128)}), f32[16,9,1024]{2,1,0:T(8,128)S(1)}, u32[]{:S(2)}, u32[]{:S(2)}) async-start(f32[16,9,1024]{2,1,0:T(8,128)} %broadcast_select_fusion), calls=%async_computation.1 | async-start | bytes 2097152 | tf_op jit(solution)/shard_map/all_to_all | solution.py:163
  31.2 5.0 %sort.17 = (s32[2048]{0:T(1024)}, s32[2048]{0:T(1024)S(1)}) sort(s32[2048]{0:T(1024)S(1)} %bitcast.245, s32[2048]{0:T(1024)S(1)} %iota.50), dimensions={0}, to_apply=%region_0.1 | sort | flops 22528 | bytes 32768 | tf_op jit(solution)/shard_map/jit(argsort)/sort | solution.py:202
  36.2 11.8 %gather_fusion = s32[2048]{0:T(1024)S(1)} fusion(s32[2048]{0:T(1024)S(1)} %bitcast.246, s32[2048]{0:T(1024)S(1)} %get-tuple-element.187), kind=kCustom, calls=%fused_computation | custom fusion | bytes 24576 | tf_op jit(solution)/shard_map/gather | solution.py:203
  48.0 4.3 %compare_select_fusion.2 = (s32[2048,1]{0,1:T(1,128)S(1)}, s32[2048,1]{0,1:T(1,128)S(1)}) fusion(s32[]{:T(128)} %bitcast.12, s32[]{:T(128)} %bitcast.13, s32[]{:T(128)} %bitcast.14, s32[]{:T(128)} %bitcast.15, s32[]{:T(128)} %bitcast.16, s32[]{:T(128)} %bitcast.18, s32[]{:T(128)} %bitcast.17, s32[2048,1]{0,1:T(1,128)S(1)} %bitcast.257), kind=kLoop, calls=%fused_computation.144 | loop fusion | flops 30720 | bytes 24604 | tf_op jit(solution)/shard_map/gather | solution.py:204
  52.6 5.7 %fusion.81 = s32[2048]{0:T(1024)S(1)} fusion(pred[2048]{0:T(1024)(128)(4,1)S(1)} %get-tuple-element.131, pred[2048]{0:T(1024)(128)(4,1)S(1)} %get-tuple-element.130, pred[2048]{0:T(1024)(128)(4,1)S(1)} %get-tuple-element.129, pred[2048]{0:T(1024)(128)(4,1)S(1)} %get-tuple-element.128, pred[2048]{0:T(1024)(128)(4,1)S(1)} %get-tuple-element.127, ...), kind=kLoop, calls=%fused_computation.192 | loop fusion | flops 24576 | bytes 43044 | tf_op jit(solution)/shard_map/add | solution.py:208
  58.2 8.0 %scatter_custom_fusion = s32[2048]{0:T(1024)S(1)} fusion(s32[2048]{0:T(1024)S(1)} %get-tuple-element.188, s32[2048]{0:T(1024)S(1)} %fusion.81, s32[]{:T(128)} %constant.279.clone.1), kind=kCustom, calls=%fused_computation.213 | custom fusion | bytes 8196 | tf_op jit(solution)/shard_map/scatter | solution.py:208
  66.3 8.8 %scatter_custom_fusion.1 = s32[4096]{0:T(1024)} fusion(s32[2048]{0:T(1024)S(1)} %compare_select_fusion.9, s32[2048]{0:T(1024)} %param.20, s32[]{:T(128)} %constant.279.clone.1), kind=kCustom, calls=%fused_computation.200 | custom fusion | bytes 16896 | tf_op jit(solution)/shard_map/scatter | solution.py:212
  75.8 6.0 %all-to-all-start = ((s32[1,16,256]{2,0,1:T(1,128)}), s32[1,16,256]{2,0,1:T(1,128)S(1)}, u32[]{:S(2)}, u32[]{:S(2)}) async-start(s32[1,16,256]{2,0,1:T(1,128)} %bitcast.20), calls=%async_computation | async-start | bytes 32768 | tf_op jit(solution)/shard_map/all_to_all | solution.py:221
  82.5 20.8 %while.15 = (s32[]{:T(128)}, f32[8,8,512]{2,1,0:T(8,128)S(1)}, s32[8,8,512]{2,1,0:T(8,128)}, f32[72,128]{1,0:T(8,128)S(1)}, s32[]{:T(128)}) while((s32[]{:T(128)}, f32[8,8,512]{2,1,0:T(8,128)S(1)}, s32[8,8,512]{2,1,0:T(8,128)}, f32[72,128]{1,0:T(8,128)S(1)}, s32[]{:T(128)}) %tuple.91), condition=%wide.region_11.12_spmd.clone, body=%wide.region_9.11_spmd.clone.sunk | while | flops 454926336 | bytes 266309 | solution.py:124
  83.3 1.8 fusion.136
  85.9 1.8 fusion.136
  103.8 3.8 %collective-permute-start = (f32[2,16,512]{2,1,0:T(8,128)S(1)}, f32[2,16,512]{2,1,0:T(8,128)S(1)}, u32[]{:S(2)}, u32[]{:S(2)}) collective-permute-start(f32[2,16,512]{2,1,0:T(8,128)S(1)} %get-tuple-element.179), channel_id=1, source_target_pairs={{0,2},{2,4},{4,6},{6,8},{8,10},{10,12},{12,14},{1,3},{3,5},{5,7},{... | collective-permute-start | bytes 196616 | tf_op jit(solution)/shard_map/ppermute | solution.py:23
  109.5 4.3 %collective-permute-done.1 = f32[2,16,512]{2,1,0:T(8,128)S(1)} collective-permute-done((f32[2,16,512]{2,1,0:T(8,128)S(1)}, f32[2,16,512]{2,1,0:T(8,128)S(1)}, u32[]{:S(2)}, u32[]{:S(2)}) %collective-permute-start.1) | collective-permute-done | bytes 65568 | tf_op jit(solution)/shard_map/ppermute | solution.py:24
  119.5 2.4 copy.63
  121.9 2.8 reshape.876
  131.7 2.3 fusion.116
  142.3 4.5 %reshape_reshape.3 = f32[2,16,4,128,4]{4,3,2,1,0:T(8,128)} reshape(f32[2,2,32,16,32]{4,3,2,1,0:T(8,128)S(1)} %bitcast.249) | data formatting | bytes 524288 | tf_op jit(solution)/shard_map/reshape;reshape | solution.py:192
  146.8 4.0 %reduce_sum.77 = f32[2,16,128]{2,1,0:T(8,128)S(1)} reduce(f32[2,16,4,128,4]{4,3,2,1,0:T(8,128)} %reshape_reshape.3, f32[]{:T(128)} %constant.278.clone.1), dimensions={2,4}, to_apply=%region_13.14 | reduce | flops 61440 | bytes 278532 | tf_op jit(solution)/shard_map/reduce_sum | solution.py:193
  151.3 6.2 %scatter_custom_fusion.2 = f32[6,4096]{0,1:T(8,128)S(1)} fusion(s32[2048]{0:T(1024)} %copy-done.7, f32[2048,6]{1,0:T(8,128)S(1)} %copy.65, f32[]{:T(128)} %constant.278.clone.1), kind=kCustom, calls=%fused_computation.68 | custom fusion | bytes 98816 | tf_op jit(solution)/shard_map/scatter | solution.py:211
  158.8 5.6 %all-to-all-start.2 = ((f32[6,16,256]{2,0,1:T(8,128)}), f32[6,16,256]{2,0,1:T(8,128)S(1)}, u32[]{:S(2)}, u32[]{:S(2)}) async-start(f32[6,16,256]{2,0,1:T(8,128)} %copy.66), calls=%async_computation.2 | async-start | bytes 262144 | tf_op jit(solution)/shard_map/all_to_all | solution.py:214
  164.4 7.8 %all-to-all-done.2 = f32[6,16,256]{2,0,1:T(8,128)S(1)} async-done(((f32[6,16,256]{2,0,1:T(8,128)}), f32[6,16,256]{2,0,1:T(8,128)S(1)}, u32[]{:S(2)}, u32[]{:S(2)}) %all-to-all-start.2) | async-done | bytes 98336 | tf_op jit(solution)/shard_map/all_to_all | solution.py:214
  172.9 5.1 %copy.68 = f32[16384,3]{1,0:T(8,128)} copy(f32[16384,3]{0,1:T(4,128)S(1)} %maximum_bitcast_fusion.1) | data formatting | bytes 393216 | tf_op jit(solution)/shard_map/stack | solution.py:235
  178.0 106.4 %scatter_custom_fusion.3 = f32[3,2193]{0,1:T(8,128)S(1)} fusion(s32[16384]{0:T(1024)S(1)} %bitcast.260, f32[16384,3]{1,0:T(8,128)} %copy.68, f32[]{:T(128)} %constant.278.clone.1), kind=kCustom, calls=%fused_computation.71 | custom fusion | flops 49152 | bytes 26828 | tf_op jit(solution)/shard_map/scatter-add | solution.py:238
  (172 shorter events, 54.3 us)
Async XLA Ops:
  0.0 24.3 %copy-start = (f32[8,8,1024]{2,1,0:T(8,128)S(1)}, f32[8,8,1024]{2,1,0:T(8,128)}, u32[]{:S(2)}) copy-start(f32[8,8,1024]{2,1,0:T(8,128)} %param.16) | copy-start | bytes 786436
  25.3 4.8 %copy-start.2 = (s32[2048,1]{0,1:T(1,128)S(1)}, s32[2048,1]{0,1:T(1,128)}, u32[]{:S(2)}) copy-start(s32[2048,1]{0,1:T(1,128)} %param.19) | copy-start | bytes 24580
  26.4 49.4 %all-to-all-start.1 = ((f32[16,9,1024]{2,1,0:T(8,128)}), f32[16,9,1024]{2,1,0:T(8,128)S(1)}, u32[]{:S(2)}, u32[]{:S(2)}) async-start(f32[16,9,1024]{2,1,0:T(8,128)} %broadcast_select_fusion), calls=%async_computation.1 | async-start | bytes 2097152 | tf_op jit(solution)/shard_map/all_to_all | solution.py:163
  36.2 38.9 %copy-start.8 = (s32[1,9]{1,0:T(1,128)S(1)}, s32[1,9]{1,0:T(1,128)}, u32[]{:S(2)}) copy-start(s32[1,9]{1,0:T(1,128)} %param.17) | copy-start | bytes 112
  66.3 15.5 %copy-start.7 = (s32[2048]{0:T(1024)}, s32[2048]{0:T(1024)S(1)}, u32[]{:S(2)}) copy-start(s32[2048]{0:T(1024)S(1)} %compare_select_fusion.9) | copy-start | bytes 24580
  75.8 33.2 %all-to-all-start = ((s32[1,16,256]{2,0,1:T(1,128)}), s32[1,16,256]{2,0,1:T(1,128)S(1)}, u32[]{:S(2)}, u32[]{:S(2)}) async-start(s32[1,16,256]{2,0,1:T(1,128)} %bitcast.20), calls=%async_computation | async-start | bytes 32768 | tf_op jit(solution)/shard_map/all_to_all | solution.py:221
  82.5 20.8 %copy-start.3 = (f32[2,64,512]{2,1,0:T(8,128)S(1)}, f32[2,64,512]{2,1,0:T(8,128)}, u32[]{:S(2)}) copy-start(f32[2,64,512]{2,1,0:T(8,128)} %param.14) | copy-start | bytes 786436
  82.5 20.8 %copy-start.4 = (f32[64,512]{1,0:T(8,128)S(1)}, f32[64,512]{1,0:T(8,128)}, u32[]{:S(2)}) copy-start(f32[64,512]{1,0:T(8,128)} %param.15) | copy-start | bytes 393220
  103.8 5.7 %collective-permute-start = (f32[2,16,512]{2,1,0:T(8,128)S(1)}, f32[2,16,512]{2,1,0:T(8,128)S(1)}, u32[]{:S(2)}, u32[]{:S(2)}) collective-permute-start(f32[2,16,512]{2,1,0:T(8,128)S(1)} %get-tuple-element.179), channel_id=1, source_target_pairs={{0,2},{2,4},{4,6},{6,8},{8,10},{10,12},{12,14},{1,3},{3,5},{5,7},{... | collective-permute-start | bytes 196616 | tf_op jit(solution)/shard_map/ppermute | solution.py:23
  107.7 6.2 %collective-permute-start.1 = (f32[2,16,512]{2,1,0:T(8,128)S(1)}, f32[2,16,512]{2,1,0:T(8,128)S(1)}, u32[]{:S(2)}, u32[]{:S(2)}) collective-permute-start(f32[2,16,512]{2,1,0:T(8,128)S(1)} %get-tuple-element.180), channel_id=1, source_target_pairs={{2,0},{4,2},{6,4},{8,6},{10,8},{12,10},{14,12},{3,1},{5,3},{7,5},{... | collective-permute-start | bytes 196616 | tf_op jit(solution)/shard_map/ppermute | solution.py:24
  113.9 3.2 %collective-permute-start.2 = (f32[2,96,16]{2,1,0:T(8,128)S(1)}, f32[2,96,16]{2,1,0:T(8,128)S(1)}, u32[]{:S(2)}, u32[]{:S(2)}) collective-permute-start(f32[2,96,16]{2,1,0:T(8,128)S(1)} %get-tuple-element.177), channel_id=1, source_target_pairs={{0,1},{2,3},{4,5},{6,7},{8,9},{10,11},{12,13},{14,15},{16,17},{18,... | collective-permute-start | bytes 36872 | tf_op jit(solution)/shard_map/ppermute | solution.py:23
  115.2 3.2 %collective-permute-start.3 = (f32[2,96,16]{2,1,0:T(8,128)S(1)}, f32[2,96,16]{2,1,0:T(8,128)S(1)}, u32[]{:S(2)}, u32[]{:S(2)}) collective-permute-start(f32[2,96,16]{2,1,0:T(8,128)S(1)} %get-tuple-element.178), channel_id=1, source_target_pairs={{1,0},{3,2},{5,4},{7,6},{9,8},{11,10},{13,12},{15,14},{17,16},{19,... | collective-permute-start | bytes 36872 | tf_op jit(solution)/shard_map/ppermute | solution.py:24
  146.8 4.1 %copy-start.6 = (f32[4,2048]{1,0:T(4,128)S(1)}, f32[4,2048]{1,0:T(4,128)}, u32[]{:S(2)}) copy-start(f32[4,2048]{1,0:T(4,128)} %param.21) | copy-start | bytes 98308
  151.3 13.1 %copy-start.5 = (s32[4096]{0:T(1024)S(1)}, s32[4096]{0:T(1024)}, u32[]{:S(2)}) copy-start(s32[4096]{0:T(1024)} %get-tuple-element.186) | copy-start | bytes 49156
  158.8 13.5 %all-to-all-start.2 = ((f32[6,16,256]{2,0,1:T(8,128)}), f32[6,16,256]{2,0,1:T(8,128)S(1)}, u32[]{:S(2)}, u32[]{:S(2)}) async-start(f32[6,16,256]{2,0,1:T(8,128)} %copy.66), calls=%async_computation.2 | async-start | bytes 262144 | tf_op jit(solution)/shard_map/all_to_all | solution.py:214
  172.9 117.9 %copy-start.1 = (f32[8,8,1024]{2,1,0:T(8,128)S(1)}, f32[8,8,1024]{2,1,0:T(8,128)}, u32[]{:S(2)}) copy-start(f32[8,8,1024]{2,1,0:T(8,128)} %param.16) | copy-start | bytes 786436
  285.0 2.1 collective-permute-start.4
  287.4 2.6 collective-permute-start.5
where the time goes:
time: 294 us; the launch traced here: 291 us
  other arithmetic  138 us (47%)
  local copies, waits for them, and re-layouts  65.9 us (22%)
  starting transfers between devices  25.5 us (9%)
  blocking collectives  23.3 us (8%)
  matrix products  21.5 us (7%)
  waiting for transfers between devices  16 us (5%)
    scatter-add x1, other arithmetic, body(): jnp.zeros((3, (map_lat + 1) * stride), jnp.float32).at[:, corners]  106 us
    all_gather x1, blocking collectives, body(): lax.all_gather(radar_parcel_listing, ('az', 'rg'), axis=0, tiled=True)  23.3 us
    dot_general x8, matrix products, lookup_block(): jnp.dot(selector, table_rows, precision=HIGH, preferred_element_type=jnp....  14.3 us
    gather x1, local copies, waits for them, and re-layouts, body(): sorted_owner = owner_tile[sort_order]  11.8 us
    scatter x1, local copies, waits for them, and re-layouts, body(): jnp.zeros((tiles * capacity,), jnp.int32).at[slot_index]  8.79 us
    scatter x1, local copies, waits for them, and re-layouts, body(): slot_index = jnp.zeros((look_total,), jnp.int32).at[sort_order].set(sorte...  8.05 us
    all_to_all x1, waiting for transfers between devices, body(): lax.all_to_all(payload_buffer.reshape(6, tiles, capacity), ('az', 'rg'),...  7.85 us
    scatter x1, local copies, waits for them, and re-layouts, body(): jnp.zeros((6, tiles * capacity), jnp.float32).at[:, slot_index].set(payload)  6.22 us
  transfers between devices with their start and end apart: 9, of which 6 were waited for; matrix products, arithmetic and copies ran while one was open for 23% of the time, Pallas kernels for 0%

commit v1 on v0

v1 whole, which is shorter than its diff:
```python
import functools
import math

import jax
import jax.numpy as jnp
import numpy as np
from jax import lax
from jax.experimental import pallas as pl
from jax.experimental.pallas import tpu as pltpu
from jax.sharding import PartitionSpec as P

PATCH = 64
LOOK = 4
LANES = 128
EPS = 1e-06
F32 = jnp.float32
BF16 = jnp.bfloat16


def padded_2(value, sides, width):
    for axis, dim in sides:
        size, length = (lax.axis_size(axis), value.shape[dim])
        up = [(i, (i + 1) % size) for i in range(size - 1)]
        down = [(j, i) for i, j in up]
        last = lax.slice_in_dim(value, length - width, length, axis=dim)
        first = lax.slice_in_dim(value, 0, width, axis=dim)
        before = lax.ppermute(last, axis, up)
        after = lax.ppermute(first, axis, down)
        value = jnp.concatenate([before, value, after], axis=dim)
    return value


def block_coords(block_lists, nlon_count):
    clipped = jnp.maximum(block_lists, 0)
    return (clipped // nlon_count, clipped % nlon_count)


def entry_rank(owner_key, is_valid):
    slots = owner_key.shape[-1]
    same_owner = (owner_key[:, :, None] == owner_key[:, None, :]) & is_valid[:, None, :]
    slot_ids = jnp.arange(slots, dtype=jnp.int32)
    earlier = slot_ids[None, :] < slot_ids[:, None]
    return jnp.sum((same_owner & earlier[None]).astype(jnp.int32), axis=2)


def pack_blocks(block_lists, owner_key, local_block, source_rows, self_key):
    slots = block_lists.shape[-1]
    is_valid = block_lists >= 0
    rank_within = entry_rank(owner_key, is_valid)
    slot_ids = jnp.arange(slots, dtype=jnp.int32)
    matches = (is_valid & (owner_key == self_key))[:, :, None] & (
        rank_within[:, :, None] == slot_ids[None, None, :]
    )
    picked = jnp.sum(jnp.where(matches, local_block[:, :, None], 0), axis=1)
    present = jnp.any(matches, axis=1)
    return jnp.where(present[..., None], source_rows[picked], 0.0)


def unpack_blocks(own_list, owner_key, received):
    slots = own_list.shape[-1]
    is_valid = own_list >= 0
    rank_within = entry_rank(owner_key[None], is_valid[None])[0]
    position = jnp.where(is_valid, owner_key * slots + rank_within, 0)
    return received.reshape(-1, received.shape[-1])[position]


def halves(value):
    high = value.astype(BF16)
    return high, (value - high.astype(F32)).astype(BF16)


def dot3(left, right):
    left_high, left_low = left
    right_high, right_low = right
    out = jnp.dot(left_high, right_high, preferred_element_type=F32)
    out = out + jnp.dot(left_low, right_high, preferred_element_type=F32)
    return out + jnp.dot(left_high, right_low, preferred_element_type=F32)


def filter_tables():
    steps = np.arange(PATCH)
    angle = (steps[:, None] * steps[None, :] % PATCH) * (2.0 * math.pi / PATCH)
    cosine, sine = np.cos(angle), np.sin(angle)
    left = np.block([[cosine, sine], [-sine, cosine]])
    step, wide = PATCH // 2, 4 * PATCH
    right = np.zeros((2 * wide, 2 * wide))
    for p in range(4):
        rows, cols = slice(p * step, p * step + PATCH), slice(p * PATCH, (p + 1) * PATCH)
        rows_im = slice(wide + p * step, wide + p * step + PATCH)
        cols_im = slice(wide + p * PATCH, wide + (p + 1) * PATCH)
        right[rows, cols] = cosine
        right[rows, cols_im] = -sine
        right[rows_im, cols] = sine
        right[rows_im, cols_im] = cosine
    group = np.arange(wide) // PATCH
    same = group[:, None] == group[None, :]
    gap = (np.arange(wide)[:, None] - np.arange(wide)[None, :]) % PATCH
    band = same & ((gap <= 1) | (gap == PATCH - 1))
    cells = PATCH // 2 // LOOK
    places = PATCH // 4 + np.arange(cells * LOOK)
    turn = steps[:, None] * places[None, :] % PATCH * (2.0 * math.pi / PATCH)
    mean_re = np.cos(turn).reshape(PATCH, cells, LOOK).mean(axis=2) / PATCH
    mean_im = np.sin(turn).reshape(PATCH, cells, LOOK).mean(axis=2) / PATCH
    back_left = np.block([[mean_re.T, -mean_im.T], [mean_im.T, mean_re.T]])
    back_right = np.zeros((2 * wide, 8 * cells))
    for p in range(4):
        rows = slice(p * PATCH, (p + 1) * PATCH)
        rows_im = slice(wide + p * PATCH, wide + (p + 1) * PATCH)
        cols = slice(p * cells, (p + 1) * cells)
        cols_im = slice((4 + p) * cells, (5 + p) * cells)
        back_right[rows, cols] = mean_re
        back_right[rows, cols_im] = mean_im
        back_right[rows_im, cols] = -mean_im
        back_right[rows_im, cols_im] = mean_re
    tables = []
    for table in (left, right, back_left, back_right):
        high = table.astype(np.float32).astype(jnp.bfloat16)
        tables += [high, (table - high.astype(np.float64)).astype(jnp.bfloat16)]
    return tables + [band.astype(jnp.bfloat16), same.astype(jnp.bfloat16)]


def sine_cosine(angle):
    turns = jnp.floor(angle * (2.0 / math.pi) + 0.5)
    rest = angle - turns * 1.5703125
    rest = rest - turns * 4.837512969970703e-04
    rest = rest - turns * 7.549789948768648e-08
    square = rest * rest
    sine = ((-1.9515295891e-4 * square + 8.3321608736e-3) * square - 1.6666654611e-1) * square
    sine = sine * rest + rest
    cosine = ((2.443315711809948e-5 * square - 1.388731625493765e-3) * square + 4.166664568298827e-2)
    cosine = cosine * square * square - 0.5 * square + 1.0
    quarter = turns.astype(jnp.int32) & 3
    swap = (quarter & 1) == 1
    sine_out = jnp.where(swap, cosine, sine)
    cosine_out = jnp.where(swap, sine, cosine)
    sine_out = jnp.where(quarter >= 2, -sine_out, sine_out)
    cosine_out = jnp.where((quarter == 1) | (quarter == 2), -cosine_out, cosine_out)
    return sine_out, cosine_out


def flatten_tile(image_ref, factor_ref, position_ref, table_ref, flat_ref):
    lines, samples = factor_ref.shape
    slots, parcel = table_ref.shape
    for column in range(samples // LANES):
        span = slice(column * LANES, (column + 1) * LANES)
        position = position_ref[:, span]
        lane = position & (LANES - 1)
        row = lax.shift_right_logical(position, LANES.bit_length() - 1)

        heights = jnp.zeros((lines, LANES), F32)
        for slot in range(slots):
            for part in range(parcel // LANES):
                source = table_ref[slot : slot + 1, part * LANES : (part + 1) * LANES]
                picked = jnp.take_along_axis(
                    jnp.broadcast_to(source, (lines, LANES)), lane, axis=1
                )
                heights = jnp.where(row == slot * (parcel // LANES) + part, picked, heights)
        sine, cosine = sine_cosine(factor_ref[:, span] * heights)
        real, imag = image_ref[0, :, span], image_ref[1, :, span]
        flat_ref[0, :, span] = real * cosine + imag * sine
        flat_ref[1, :, span] = imag * cosine - real * sine


def goldstein_looks(padded, tables):
    left = (tables[0][...], tables[1][...])
    right = (tables[2], tables[3])
    back_left = (tables[4][...], tables[5][...])
    back_right = (tables[6], tables[7])
    band, same = tables[8][...], tables[9][...]
    step, wide = PATCH // 2, 4 * PATCH
    lines, samples = padded.shape[1:]
    block_rows = (lines - step) // step
    groups = (samples - LANES) // LANES
    columns = []
    for u in range(block_rows):
        strip = jnp.concatenate(
            [padded[0, u * step : u * step + PATCH], padded[1, u * step : u * step + PATCH]], axis=0
        )
        columns.append(dot3(left, halves(strip)))
    real = halves(jnp.concatenate([c[:PATCH] for c in columns], axis=0))
    imag = halves(jnp.concatenate([c[PATCH:] for c in columns], axis=0))
    rows_re, rows_im = [], []
    for q in range(groups):
        window = slice(q * LANES, q * LANES + wide)
        spectrum = dot3(
            (real[0][:, window], real[1][:, window]), (right[0][:wide], right[1][:wide])
        ) + dot3((imag[0][:, window], imag[1][:, window]), (right[0][wide:], right[1][wide:]))
        spec_re, spec_im = spectrum[:, :wide], spectrum[:, wide:]
        size = jnp.sqrt(spec_re * spec_re + spec_im * spec_im)
        size_high, size_low = halves(size)
        across = jnp.dot(size_high, band, preferred_element_type=F32) + jnp.dot(
            size_low, band, preferred_element_type=F32
        )
        gains = []
        for u in range(block_rows):
            part = across[u * PATCH : (u + 1) * PATCH]
            around = part + pltpu.roll(part, 1, 0) + pltpu.roll(part, PATCH - 1, 0)
            column = jnp.sum(size[u * PATCH : (u + 1) * PATCH], axis=0, keepdims=True)
            column_high, column_low = halves(jnp.broadcast_to(column, (16, wide)))
            total = jnp.dot(column_high, same, preferred_element_type=F32) + jnp.dot(
                column_low, same, preferred_element_type=F32
            )
            scale = (1.0 / 9.0) / (total[:1] * (1.0 / PATCH**2) + EPS)
            gains.append(jnp.sqrt(around * scale))
        gain = jnp.concatenate(gains, axis=0)
        rows = dot3(halves(spec_re * gain), (back_right[0][:wide], back_right[1][:wide])) + dot3(
            halves(spec_im * gain), (back_right[0][wide:], back_right[1][wide:])
        )
        half = rows.shape[1] // 2
        rows_re.append(rows[:, :half])
        rows_im.append(rows[:, half:])
    rows_re = jnp.concatenate(rows_re, axis=1)
    rows_im = jnp.concatenate(rows_im, axis=1)
    looks = []
    for u in range(block_rows):
        rows = slice(u * PATCH, (u + 1) * PATCH)
        looks.append(dot3(back_left, halves(jnp.concatenate([rows_re[rows], rows_im[rows]], axis=0))))
    half = looks[0].shape[0] // 2
    return [jnp.concatenate([x[:half] for x in looks], axis=0), jnp.concatenate([x[half:] for x in looks], axis=0)]


def place_looks(owner_ref, base_ref, share_ref, row_ref, hit_ref, map_lat, map_lon, tile_lat, tile_lon):
    chunks = owner_ref.shape[0]
    count_rg = map_lon // tile_lon
    owner, base = owner_ref[...], base_ref[...]
    anchor_row = owner // count_rg * tile_lat + base // tile_lon
    anchor_col = owner % count_rg * tile_lon + base % tile_lon
    row_ids = lax.broadcasted_iota(jnp.int32, (map_lat, LANES), 0)
    col_ids = lax.broadcasted_iota(jnp.int32, (map_lon, LANES), 0)
    for i in range(chunks):
        span = slice(i * LANES, (i + 1) * LANES)
        hit_ref[:, span] = (col_ids == anchor_col[i : i + 1]).astype(F32).astype(BF16)
        gap = row_ids - anchor_row[i : i + 1]
        for c in range(2):
            upper, lower = share_ref[c, i : i + 1, :], share_ref[2 + c, i : i + 1, :]
            row_ref[c, :, span] = jnp.where(gap == 0, upper, jnp.where(gap == 1, lower, 0.0))


def splat(row_ref, hit_ref, look):
    dims = (((1,), (1,)), ((), ()))
    chunks = hit_ref.shape[1] // LANES
    sums = []
    for c in range(2):
        if look is None:
            value = row_ref[c]
        else:
            value = jnp.concatenate(
                [row_ref[c, :, i * LANES : (i + 1) * LANES] * look[i : i + 1] for i in range(chunks)],
                axis=1,
            )
        high, low = halves(value)
        sums.append(
            lax.dot_general(high, hit_ref[...], dims, preferred_element_type=F32)
            + lax.dot_general(low, hit_ref[...], dims, preferred_element_type=F32)
        )
    moved = pltpu.roll(sums[1], 1, 1)
    first = lax.broadcasted_iota(jnp.int32, moved.shape, 1) == 0
    return sums[0] + jnp.where(first, 0.0, moved)


def filter_kernel(tile_shape, padded_ref, owner_ref, base_ref, share_ref, *refs):
    tables, (out_ref, row_ref, hit_ref) = refs[:10], refs[10:]
    map_lat, map_lon = out_ref.shape[1:]
    place_looks(owner_ref, base_ref, share_ref, row_ref, hit_ref, map_lat, map_lon, *tile_shape)
    looks = goldstein_looks(padded_ref, tables)
    out_ref[0] = splat(row_ref, hit_ref, looks[0])
    out_ref[1] = splat(row_ref, hit_ref, looks[1])
    out_ref[2] = splat(row_ref, hit_ref, None)


def body(
    complex_phase_image,
    phase_to_topography_factor,
    terrain_model_heights,
    radar_parcel_listing,
    pixel_terrain_position,
    multilook_receiving_patch,
    multilook_base_point,
    multilook_splat_shares,
):
    count_az = lax.axis_size("az")
    count_rg = lax.axis_size("rg")
    self_az = lax.axis_index("az")
    self_rg = lax.axis_index("rg")
    parcel_north_coordinate, parcel_east_coordinate, number_terrain_points = (
        terrain_model_heights.shape
    )
    nlon_count = parcel_east_coordinate * count_rg
    own_list = radar_parcel_listing[0]
    lat_own, lon_own = block_coords(own_list, nlon_count)
    all_lists = lax.all_gather(radar_parcel_listing, ("az", "rg"), axis=0, tiled=True)
    lat_all, lon_all = block_coords(all_lists, nlon_count)
    key_all = lat_all // parcel_north_coordinate * count_rg + lon_all // parcel_east_coordinate
    local_all = (lat_all - self_az * parcel_north_coordinate) * parcel_east_coordinate + (
        lon_all - self_rg * parcel_east_coordinate
    )
    outgoing = pack_blocks(
        all_lists,
        key_all,
        local_all,
        terrain_model_heights.reshape(
            parcel_north_coordinate * parcel_east_coordinate, number_terrain_points
        ),
        self_az * count_rg + self_rg,
    )
    received = lax.all_to_all(outgoing, ("az", "rg"), split_axis=0, concat_axis=0, tiled=True)
    key_own = lat_own // parcel_north_coordinate * count_rg + lon_own // parcel_east_coordinate
    height_lookup_table = unpack_blocks(own_list, key_own, received)
    az_lines, rg_samples = phase_to_topography_factor.shape
    flattened = pl.pallas_call(
        flatten_tile,
        out_shape=jax.ShapeDtypeStruct((2, az_lines, rg_samples), F32),
        name="flatten",
    )(complex_phase_image, phase_to_topography_factor, pixel_terrain_position, height_lookup_table)
    rim = PATCH // 4
    padded = padded_2(flattened, (("az", 1), ("rg", 2)), rim)
    padded = jnp.pad(padded, ((0, 0), (0, 0), (0, LANES - 2 * rim)))
    map_lat = az_lines // LOOK
    map_lon = rg_samples // LOOK
    chunks = map_lat * map_lon // LANES
    tables = filter_tables()
    sums = pl.pallas_call(
        functools.partial(filter_kernel, (map_lat, map_lon)),
        out_shape=jax.ShapeDtypeStruct((3, map_lat * count_az, map_lon * count_rg), F32),
        scratch_shapes=[
            pltpu.VMEM((2, map_lat * count_az, chunks * LANES), F32),
            pltpu.VMEM((map_lon * count_rg, chunks * LANES), BF16),
        ],
        compiler_params=pltpu.CompilerParams(vmem_limit_bytes=48 * 1024 * 1024),
        name="filter_splat",
    )(
        padded,
        multilook_receiving_patch.reshape(chunks, LANES),
        multilook_base_point.reshape(chunks, LANES),
        multilook_splat_shares.reshape(4, chunks, LANES),
        *tables,
    )
    sums = lax.psum_scatter(sums, "rg", scatter_dimension=2, tiled=True)
    sums = lax.psum_scatter(sums, "az", scatter_dimension=1, tiled=True)
    return sums[:2] / jnp.maximum(sums[2:3], 1.0)


def solution(mesh):
    return jax.shard_map(
        body,
        mesh=mesh,
        in_specs=(
            P(None, ("scene", "az"), "rg"),
            P(("scene", "az"), "rg"),
            P(("scene", "az"), "rg", None),
            P(("scene", "az", "rg"), None),
            P(("scene", "az"), "rg"),
            P(("scene", "az", "rg"), None),
            P(("scene", "az", "rg")),
            P(None, ("scene", "az", "rg")),
        ),
        out_specs=P(None, ("scene", "az"), "rg"),
        check_vma=False,
    )
```

time: 294 us -> 181 us (0.62)
  other arithmetic: 138 us -> 4.42 us
  waiting for transfers between devices: 16 us -> 105 us
  local copies, waits for them, and re-layouts: 65.9 us -> 4.81 us
  matrix products: 21.5 us -> 0 us
  Pallas kernels: 0 us -> 17.6 us
  starting transfers between devices: 25.5 us -> 12.1 us
  between operations: 0.74 us -> 13.8 us
    scatter-add x1 -> x0, other arithmetic: 106 us -> none  [body(): jnp.zeros((3, (map_lat + 1) * stride), jnp.float32).at[:, corners]]
    reduce_scatter x0 -> x2, waiting for transfers between devices: none -> 74.3 us  [the longest x1 66 us: body(): sums = lax.psum_scatter(sums, 'az', scatter_dimension=1, tiled=True)]
    scatter x3 -> x0, local copies, waits for them, and re-layouts: 23.1 us -> none  [the longest x1 8.79 us: body(): jnp.zeros((tiles * capacity,), jnp.int32).at[slot_index]]
    all_to_all x1, waiting for transfers between devices: 0.01 us -> 22.5 us  [body(): lax.all_to_all(outgoing, ('az', 'rg'), split_axis=0, concat_axis=0, tiled...]
    dot_general x14 -> x0, matrix products: 21.5 us -> none  [the longest x8 14.3 us: lookup_block(): jnp.dot(selector, table_rows, precision=HIGH, preferred_element_type=jnp....]
    pallas_call x0 -> x2, Pallas kernels: none -> 17.6 us  [the longest x1 9.24 us: body(): pl.pallas_call(functools.partial(filter_kernel, (map_lat, map_lon)), out_...]
    gather x2 -> x0, local copies, waits for them, and re-layouts: 12.5 us -> none  [the longest x1 11.8 us: body(): sorted_owner = owner_tile[sort_order]]
    all_to_all x2 -> x0, starting transfers between devices: 11.5 us -> none  [the longest x1 5.98 us: body(): lax.all_to_all(cell_buffer.reshape(1, tiles, capacity), ('az', 'rg'), spl...]
  transfers between devices with their start and end apart: 9 -> 7, of which waited for: 6 -> 6; matrix products, arithmetic and copies ran while one was open for 23% -> 0% of each run, Pallas kernels for 0% -> 0%
where the time goes in v1:
time: 181 us; the launch traced here: 180 us
  waiting for transfers between devices  105 us (58%)
  blocking collectives  23 us (13%)
  Pallas kernels  17.6 us (10%)
  between operations  13.8 us (8%)
  starting transfers between devices  12.1 us (7%)
  local copies, waits for them, and re-layouts  4.81 us (3%)
  other arithmetic  4.42 us (2%)
    reduce_scatter x1, waiting for transfers between devices, body(): sums = lax.psum_scatter(sums, 'az', scatter_dimension=1, tiled=True)  66 us
    all_gather x1, blocking collectives, body(): lax.all_gather(radar_parcel_listing, ('az', 'rg'), axis=0, tiled=True)  23 us
    all_to_all x1, waiting for transfers between devices, body(): lax.all_to_all(outgoing, ('az', 'rg'), split_axis=0, concat_axis=0, tiled...  22.5 us
    pallas_call x1, Pallas kernels, body(): pl.pallas_call(functools.partial(filter_kernel, (map_lat, map_lon)), out_...  9.24 us
    pallas_call x1, Pallas kernels, body(): pl.pallas_call(flatten_tile, out_shape=jax.ShapeDtypeStruct((2, az_lines,...  8.34 us
    reduce_scatter x1, waiting for transfers between devices, body(): sums = lax.psum_scatter(sums, 'rg', scatter_dimension=2, tiled=True)  8.3 us
    ppermute x2, waiting for transfers between devices, padded_2(): after = lax.ppermute(first, axis, down)  6.89 us
    ppermute x2, starting transfers between devices, padded_2(): before = lax.ppermute(last, axis, up)  5.64 us
  transfers between devices with their start and end apart: 7, of which 6 were waited for; matrix products, arithmetic and copies ran while one was open for 0% of the time, Pallas kernels for 0%

profile of v1, /device:TPU:0, one launch (start us, length us, event | category | flops | bytes accessed | tf_op | source)
XLA Modules:
  0.0 180.3 jit_solution(5370054565918936696)
XLA Ops:
  6.6 0.7 copy-done.15
  7.2 23.0 %all-gather = s32[16,1,9]{2,1,0:T(1,128)S(1)} all-gather(s32[1,1,9]{2,1,0:T(1,128)S(1)} %bitcast.120), channel_id=1, replica_groups=mesh['scene'=2,'az'=8,'rg'=2] {'az','rg'}, dimensions={0}, use_global_device_ids=true | all-gather | bytes 612 | tf_op jit(solution)/shard_map/all_gather | solution.py:291
  30.5 0.3 convert_reduce_fusion
  31.2 0.8 gather_fusion
  32.2 1.1 broadcast_select_fusion
  33.3 3.7 %all-to-all-start = ((f32[16,9,1024]{2,1,0:T(8,128)}), f32[16,9,1024]{2,1,0:T(8,128)S(1)}, u32[]{:S(2)}, u32[]{:S(2)}) async-start(f32[16,9,1024]{2,1,0:T(8,128)} %broadcast_select_fusion), calls=%async_computation | async-start | bytes 2097152 | tf_op jit(solution)/shard_map/all_to_all | solution.py:306
  37.0 0.3 fusion.17
  37.4 22.5 %all-to-all-done = f32[16,9,1024]{2,1,0:T(8,128)S(1)} async-done(((f32[16,9,1024]{2,1,0:T(8,128)}), f32[16,9,1024]{2,1,0:T(8,128)S(1)}, u32[]{:S(2)}, u32[]{:S(2)}) %all-to-all-start) | async-done | bytes 589856 | tf_op jit(solution)/shard_map/all_to_all | solution.py:306
  59.9 1.2 gather_fusion.1
  61.1 8.3 %flatten.1 = f32[2,64,512]{2,1,0:T(8,128)} custom-call(f32[2,64,512]{2,1,0:T(8,128)} %image_ref.1, f32[64,512]{1,0:T(8,128)} %factor_ref.1, s32[64,512]{1,0:T(8,128)} %position_ref.1, f32[9,1024]{1,0:T(8,128)} %gather_fusion.1), custom_call_target="tpu_custom_call" | custom-call | tf_op jit(solution)/shard_map/flatten/pallas_call | solution.py:310
  69.4 0.9 fusion.23
  70.4 3.7 %collective-permute-start = (f32[2,16,512]{2,1,0:T(8,128)S(1)}, f32[2,16,512]{2,1,0:T(8,128)S(1)}, u32[]{:S(2)}, u32[]{:S(2)}) collective-permute-start(f32[2,16,512]{2,1,0:T(8,128)S(1)} %get-tuple-element.10), channel_id=1, source_target_pairs={{0,2},{2,4},{4,6},{6,8},{8,10},{10,12},{12,14},{1,3},{3,5},{5,7},{... | collective-permute-start | bytes 196616 | tf_op jit(solution)/shard_map/ppermute | solution.py:27
  74.1 1.3 collective-permute-start.1
  75.4 1.0 collective-permute-done
  76.3 5.3 %collective-permute-done.1 = f32[2,16,512]{2,1,0:T(8,128)S(1)} collective-permute-done((f32[2,16,512]{2,1,0:T(8,128)S(1)}, f32[2,16,512]{2,1,0:T(8,128)S(1)}, u32[]{:S(2)}, u32[]{:S(2)}) %collective-permute-start.1) | collective-permute-done | bytes 65568 | tf_op jit(solution)/shard_map/ppermute | solution.py:28
  81.7 2.0 %collective-permute-start.2 = (f32[2,96,16]{2,1,0:T(8,128)S(1)}, f32[2,96,16]{2,1,0:T(8,128)S(1)}, u32[]{:S(2)}, u32[]{:S(2)}) collective-permute-start(f32[2,96,16]{2,1,0:T(8,128)S(1)} %get-tuple-element.8), channel_id=1, source_target_pairs={{0,1},{2,3},{4,5},{6,7},{8,9},{10,11},{12,13},{14,15},{16,17},{18,... | collective-permute-start | bytes 36872 | tf_op jit(solution)/shard_map/ppermute | solution.py:27
  83.7 1.5 collective-permute-start.3
  85.3 1.6 collective-permute-done.3
  87.2 0.6 copy-done.11
  87.8 9.2 %filter_splat.1 = f32[3,128,256]{2,1,0:T(8,128)} custom-call(f32[2,96,640]{2,1,0:T(8,128)S(1)} %select_maximum_fusion.padded_ref, s32[16,128]{1,0:T(8,128)S(1)} %bitcast.115, s32[16,128]{1,0:T(8,128)S(1)} %bitcast.116, f32[4,16,128]{2,1,0:T(8,128)S(1)} %bitcast.114, bf16[128,128]{1,0:T(8,128)(2,1)S(1)} %copy-done.7, bf16[128,128]{1,0:T(8,128)(2,1)S(1)} %copy-done.8, ...), custom_call_target="tpu_custom_call" | custom-call | tf_op jit(solution)/shard_map/filter_splat/pallas_call | solution.py:322
  97.1 8.3 %reduce-scatter.3.cloned.1.call-done = f32[3,128,128]{2,1,0:T(8,128)} async-done(((f32[3,128,256]{2,1,0:T(8,128)}), f32[3,128,128]{2,1,0:T(8,128)}) %reduce-scatter.3.cloned.1.call-update) | async-done | bytes 196624 | tf_op jit(solution)/shard_map/reduce_scatter | solution.py:338
  105.4 66.0 %reduce-scatter.5.cloned.1.call-done = f32[3,16,128]{2,1,0:T(8,128)} async-done(((f32[3,128,128]{2,1,0:T(8,128)}), f32[3,16,128]{2,1,0:T(8,128)}) %reduce-scatter.5.cloned.1.call-update) | async-done | bytes 24592 | tf_op jit(solution)/shard_map/reduce_scatter | solution.py:339
  171.4 0.7 fusion.11
  172.1 1.3 slice_divide_fusion
  (55 shorter events, 1.4 us)
Async XLA Ops:
  6.5 24.7 %copy-start = (f32[8,8,1024]{2,1,0:T(8,128)S(1)}, f32[8,8,1024]{2,1,0:T(8,128)}, u32[]{:S(2)}) copy-start(f32[8,8,1024]{2,1,0:T(8,128)} %param.20) | copy-start | bytes 786436
  6.5 0.7 copy-start.15
  33.3 26.6 %all-to-all-start = ((f32[16,9,1024]{2,1,0:T(8,128)}), f32[16,9,1024]{2,1,0:T(8,128)S(1)}, u32[]{:S(2)}, u32[]{:S(2)}) async-start(f32[16,9,1024]{2,1,0:T(8,128)} %broadcast_select_fusion), calls=%async_computation | async-start | bytes 2097152 | tf_op jit(solution)/shard_map/all_to_all | solution.py:306
  36.9 68.5 %reduce-scatter.3.cloned.1.call-start = ((), (), s32[]{:S(2)}) async-start(), calls=%async_computation.3 | async-start | bytes 589824 | tf_op jit(solution)/shard_map/reduce_scatter | solution.py:338
  69.4 12.2 %copy-start.13 = (f32[2,64,512]{2,1,0:T(8,128)S(1)}, f32[2,64,512]{2,1,0:T(8,128)}, u32[]{:S(2)}) copy-start(f32[2,64,512]{2,1,0:T(8,128)} %flatten.1) | copy-start | bytes 786436
  70.4 6.0 %collective-permute-start = (f32[2,16,512]{2,1,0:T(8,128)S(1)}, f32[2,16,512]{2,1,0:T(8,128)S(1)}, u32[]{:S(2)}, u32[]{:S(2)}) collective-permute-start(f32[2,16,512]{2,1,0:T(8,128)S(1)} %get-tuple-element.10), channel_id=1, source_target_pairs={{0,2},{2,4},{4,6},{6,8},{8,10},{10,12},{12,14},{1,3},{3,5},{5,7},{... | collective-permute-start | bytes 196616 | tf_op jit(solution)/shard_map/ppermute | solution.py:27
  74.1 11.1 %copy-start.14 = (f32[4,2048]{1,0:T(4,128)S(1)}, f32[4,2048]{1,0:T(4,128)}, u32[]{:S(2)}) copy-start(f32[4,2048]{1,0:T(4,128)} %param.25) | copy-start | bytes 98308
  74.1 7.5 %collective-permute-start.1 = (f32[2,16,512]{2,1,0:T(8,128)S(1)}, f32[2,16,512]{2,1,0:T(8,128)S(1)}, u32[]{:S(2)}, u32[]{:S(2)}) collective-permute-start(f32[2,16,512]{2,1,0:T(8,128)S(1)} %get-tuple-element.11), channel_id=1, source_target_pairs={{2,0},{4,2},{6,4},{8,6},{10,8},{12,10},{14,12},{3,1},{5,3},{7,5},{... | collective-permute-start | bytes 196616 | tf_op jit(solution)/shard_map/ppermute | solution.py:28
  81.6 5.5 %copy-start.3 = (bf16[512,64]{1,0:T(8,128)(2,1)S(1)}, bf16[512,64]{1,0:T(8,128)(2,1)}, u32[]{:S(2)}) copy-start(bf16[512,64]{1,0:T(8,128)(2,1)} %constant.149.clone.refs_6_) | copy-start | bytes 196612
  81.6 5.6 %copy-start.4 = (bf16[512,64]{1,0:T(8,128)(2,1)S(1)}, bf16[512,64]{1,0:T(8,128)(2,1)}, u32[]{:S(2)}) copy-start(bf16[512,64]{1,0:T(8,128)(2,1)} %constant.150.clone.refs_7_) | copy-start | bytes 196612
  81.6 5.6 %copy-start.5 = (bf16[256,256]{1,0:T(8,128)(2,1)S(1)}, bf16[256,256]{1,0:T(8,128)(2,1)}, u32[]{:S(2)}) copy-start(bf16[256,256]{1,0:T(8,128)(2,1)} %constant.151.clone.refs_8_) | copy-start | bytes 393220
  81.6 5.6 %copy-start.6 = (bf16[256,256]{1,0:T(8,128)(2,1)S(1)}, bf16[256,256]{1,0:T(8,128)(2,1)}, u32[]{:S(2)}) copy-start(bf16[256,256]{1,0:T(8,128)(2,1)} %constant.152.clone.refs_9_) | copy-start | bytes 393220
  81.6 5.6 %copy-start.9 = (s32[2048,1]{0,1:T(1,128)S(1)}, s32[2048,1]{0,1:T(1,128)}, u32[]{:S(2)}) copy-start(s32[2048,1]{0,1:T(1,128)} %param.23) | copy-start | bytes 24580
  81.6 5.6 %copy-start.10 = (s32[2048]{0:T(1024)S(1)}, s32[2048]{0:T(1024)}, u32[]{:S(2)}) copy-start(s32[2048]{0:T(1024)} %param.24) | copy-start | bytes 24580
  81.6 5.6 %copy-start.12 = (bf16[16,128]{1,0:T(8,128)(2,1)S(1)}, bf16[16,128]{1,0:T(8,128)(2,1)}, u32[]{:S(2)}) copy-start(bf16[16,128]{1,0:T(8,128)(2,1)} %constant.148.clone.refs_5_) | copy-start | bytes 12292
  81.7 3.5 %collective-permute-start.2 = (f32[2,96,16]{2,1,0:T(8,128)S(1)}, f32[2,96,16]{2,1,0:T(8,128)S(1)}, u32[]{:S(2)}, u32[]{:S(2)}) collective-permute-start(f32[2,96,16]{2,1,0:T(8,128)S(1)} %get-tuple-element.8), channel_id=1, source_target_pairs={{0,1},{2,3},{4,5},{6,7},{8,9},{10,11},{12,13},{14,15},{16,17},{18,... | collective-permute-start | bytes 36872 | tf_op jit(solution)/shard_map/ppermute | solution.py:27
  83.7 3.2 %collective-permute-start.3 = (f32[2,96,16]{2,1,0:T(8,128)S(1)}, f32[2,96,16]{2,1,0:T(8,128)S(1)}, u32[]{:S(2)}, u32[]{:S(2)}) collective-permute-start(f32[2,96,16]{2,1,0:T(8,128)S(1)} %get-tuple-element.9), channel_id=1, source_target_pairs={{1,0},{3,2},{5,4},{7,6},{9,8},{11,10},{13,12},{15,14},{17,16},{19,... | collective-permute-start | bytes 36872 | tf_op jit(solution)/shard_map/ppermute | solution.py:28
  85.2 2.0 %copy-start.8 = (bf16[128,128]{1,0:T(8,128)(2,1)S(1)}, bf16[128,128]{1,0:T(8,128)(2,1)}, u32[]{:S(2)}) copy-start(bf16[128,128]{1,0:T(8,128)(2,1)} %constant.144.clone.refs_1_) | copy-start | bytes 98308
  85.2 2.0 %copy-start.1 = (bf16[512,512]{1,0:T(8,128)(2,1)S(1)}, bf16[512,512]{1,0:T(8,128)(2,1)}, u32[]{:S(2)}) copy-start(bf16[512,512]{1,0:T(8,128)(2,1)} %constant.145.clone.refs_2_) | copy-start | bytes 1572868
  85.2 2.0 %copy-start.2 = (bf16[512,512]{1,0:T(8,128)(2,1)S(1)}, bf16[512,512]{1,0:T(8,128)(2,1)}, u32[]{:S(2)}) copy-start(bf16[512,512]{1,0:T(8,128)(2,1)} %constant.146.clone.refs_3_) | copy-start | bytes 1572868
  85.2 2.0 %copy-start.7 = (bf16[128,128]{1,0:T(8,128)(2,1)S(1)}, bf16[128,128]{1,0:T(8,128)(2,1)}, u32[]{:S(2)}) copy-start(bf16[128,128]{1,0:T(8,128)(2,1)} %constant.143.clone.refs_0_) | copy-start | bytes 98308
  87.1 0.7 copy-start.11
  97.1 74.3 %reduce-scatter.5.cloned.1.call-start = ((), (), s32[]{:S(2)}) async-start(), calls=%async_computation.4 | async-start | bytes 221184 | tf_op jit(solution)/shard_map/reduce_scatter | solution.py:339
Sparse Core Ops, SparseCore 0:
  97.2 8.1 reduce-scatter.2
  109.0 62.3 reduce-scatter.4

commit v2 on v1

--- a/solution.py
+++ b/solution.py
@@ -15,53 +15,6 @@
 EPS = 1e-06
 F32 = jnp.float32
 BF16 = jnp.bfloat16
-
-
-def padded_2(value, sides, width):
-    for axis, dim in sides:
-        size, length = (lax.axis_size(axis), value.shape[dim])
-        up = [(i, (i + 1) % size) for i in range(size - 1)]
-        down = [(j, i) for i, j in up]
-        last = lax.slice_in_dim(value, length - width, length, axis=dim)
-        first = lax.slice_in_dim(value, 0, width, axis=dim)
-        before = lax.ppermute(last, axis, up)
-        after = lax.ppermute(first, axis, down)
-        value = jnp.concatenate([before, value, after], axis=dim)
-    return value
-
-
-def block_coords(block_lists, nlon_count):
-    clipped = jnp.maximum(block_lists, 0)
-    return (clipped // nlon_count, clipped % nlon_count)
-
-
-def entry_rank(owner_key, is_valid):
-    slots = owner_key.shape[-1]
-    same_owner = (owner_key[:, :, None] == owner_key[:, None, :]) & is_valid[:, None, :]
-    slot_ids = jnp.arange(slots, dtype=jnp.int32)
-    earlier = slot_ids[None, :] < slot_ids[:, None]
-    return jnp.sum((same_owner & earlier[None]).astype(jnp.int32), axis=2)
-
-
-def pack_blocks(block_lists, owner_key, local_block, source_rows, self_key):
-    slots = block_lists.shape[-1]
-    is_valid = block_lists >= 0
-    rank_within = entry_rank(owner_key, is_valid)
-    slot_ids = jnp.arange(slots, dtype=jnp.int32)
-    matches = (is_valid & (owner_key == self_key))[:, :, None] & (
-        rank_within[:, :, None] == slot_ids[None, None, :]
-    )
-    picked = jnp.sum(jnp.where(matches, local_block[:, :, None], 0), axis=1)
-    present = jnp.any(matches, axis=1)
-    return jnp.where(present[..., None], source_rows[picked], 0.0)
-
-
-def unpack_blocks(own_list, owner_key, received):
-    slots = own_list.shape[-1]
-    is_valid = own_list >= 0
-    rank_within = entry_rank(owner_key[None], is_valid[None])[0]
-    position = jnp.where(is_valid, owner_key * slots + rank_within, 0)
-    return received.reshape(-1, received.shape[-1])[position]
 
 
 def halves(value):
@@ -140,7 +93,7 @@
 
 def flatten_tile(image_ref, factor_ref, position_ref, table_ref, flat_ref):
     lines, samples = factor_ref.shape
-    slots, parcel = table_ref.shape
+    rows = table_ref.shape[0]
     for column in range(samples // LANES):
         span = slice(column * LANES, (column + 1) * LANES)
         position = position_ref[:, span]
@@ -148,13 +101,11 @@
         row = lax.shift_right_logical(position, LANES.bit_length() - 1)
 
         heights = jnp.zeros((lines, LANES), F32)
-        for slot in range(slots):
-            for part in range(parcel // LANES):
-                source = table_ref[slot : slot + 1, part * LANES : (part + 1) * LANES]
-                picked = jnp.take_along_axis(
-                    jnp.broadcast_to(source, (lines, LANES)), lane, axis=1
-                )
-                heights = jnp.where(row == slot * (parcel // LANES) + part, picked, heights)
+        for r in range(rows):
+            picked = jnp.take_along_axis(
+                jnp.broadcast_to(table_ref[r : r + 1], (lines, LANES)), lane, axis=1, mode="promise_in_bounds"
+            )
+            heights = jnp.where(row == r, picked, heights)
         sine, cosine = sine_cosine(factor_ref[:, span] * heights)
         real, imag = image_ref[0, :, span], image_ref[1, :, span]
         flat_ref[0, :, span] = real * cosine + imag * sine
@@ -268,6 +219,229 @@
     out_ref[2] = splat(row_ref, hit_ref, None)
 
 
+MESH = pl.DeviceIdType.MESH
+
+
+def peers(count_az):
+    az, rg = lax.axis_index("az"), lax.axis_index("rg")
+    others = [{"az": lax.rem(az + d, count_az), "rg": rg} for d in range(1, count_az)]
+    return az, rg, others, {"az": az, "rg": 1 - rg}
+
+
+def greet(devices):
+    barrier = pltpu.get_barrier_semaphore()
+    for device in devices:
+        pl.semaphore_signal(barrier, inc=1, device_id=device, device_id_type=MESH)
+    pl.semaphore_wait(barrier, len(devices))
+
+
+def remote(source, target, send_sem, recv_sem, device):
+    return pltpu.make_async_remote_copy(
+        src_ref=source,
+        dst_ref=target,
+        send_sem=send_sem,
+        recv_sem=recv_sem,
+        device_id=device,
+        device_id_type=MESH,
+    )
+
+
+def terrain_kernel(
+    count_az,
+    parcel_shape,
+    list_ref,
+    terrain_ref,
+    table_ref,
+    extended,
+    edge,
+    lists,
+    lists_smem,
+    outgoing,
+    incoming,
+    edge_sems,
+    list_send,
+    list_recv,
+    block_send,
+    block_recv,
+    local_sem,
+):
+    north, east = parcel_shape
+    slots = table_ref.shape[0]
+    az, rg, others, partner = peers(count_az)
+    greet(others + [partner])
+    list_copies = [
+        remote(list_ref, lists.at[d + 1], list_send.at[d], list_recv.at[d], device)
+        for d, device in enumerate(others)
+    ]
+    for copy in list_copies:
+        copy.start()
+    for lat in range(north):
+        edge[lat] = jnp.where(rg == 0, terrain_ref[lat * east + east - 1], terrain_ref[lat * east])
+    edge_copy = remote(
+        edge, extended.at[pl.ds(north * east, north)], edge_sems.at[0], edge_sems.at[1], partner
+    )
+    edge_copy.start()
+    extended[: north * east] = terrain_ref[...]
+    extended[north * east + north] = jnp.zeros(extended.shape[1:], F32)
+    lists[0] = list_ref[...]
+    for copy in list_copies:
+        copy.wait()
+    to_smem = pltpu.make_async_copy(lists, lists_smem, local_sem)
+    to_smem.start()
+    edge_copy.wait()
+    to_smem.wait()
+
+    def pick(d, slot):
+        number = lists_smem[d, 0, slot]
+        lat = number // (2 * east) - az * north
+        lon = number % (2 * east) - rg * east
+        inside = (number >= 0) & (lat >= 0) & (lat < north)
+        at_edge = (lon < 0) | (lon >= east)
+        place = jnp.where(at_edge, north * east + lat, lat * east + lon)
+        return extended[jnp.where(inside, place, north * east + north)]
+
+    copies = []
+    for d in range(1, count_az):
+        for slot in range(slots):
+            outgoing[d - 1, slot] = pick(d, slot)
+        device = {"az": lax.rem(az + count_az - d, count_az), "rg": rg}
+        copy = remote(
+            outgoing.at[d - 1], incoming.at[d - 1], block_send.at[d - 1], block_recv.at[d - 1], device
+        )
+        copy.start()
+        copies.append(copy)
+    for slot in range(slots):
+        table_ref[slot] = pick(0, slot)
+    for d, copy in enumerate(copies):
+        copy.wait()
+        table_ref[...] += incoming[d]
+
+
+def halo_kernel(count_az, rim, flat_ref, padded_ref, top, bottom, side, top_side, bottom_side, send, recv):
+    az, rg = lax.axis_index("az"), lax.axis_index("rg")
+    lines, samples = flat_ref.shape[1:]
+    partner = {"az": az, "rg": 1 - rg}
+    above, below = az - 1, az + 1
+    barrier = pltpu.get_barrier_semaphore()
+
+    def signal(device):
+        pl.semaphore_signal(barrier, inc=1, device_id=device, device_id_type=MESH)
+
+    edge = pl.ds(pl.multiple_of((1 - rg) * (samples - LANES), LANES), LANES)
+    first, last = pl.ds(0, rim), pl.ds(lines - rim, rim)
+    side_copy = remote(flat_ref.at[:, :, edge], side, send.at[0], recv.at[0], partner)
+    up = [
+        remote(flat_ref.at[:, first, :], bottom, send.at[1], recv.at[2], {"az": above, "rg": rg}),
+        remote(
+            flat_ref.at[:, first, edge], bottom_side, send.at[2], recv.at[4], {"az": above, "rg": 1 - rg}
+        ),
+    ]
+    down = [
+        remote(flat_ref.at[:, last, :], top, send.at[3], recv.at[1], {"az": below, "rg": rg}),
+        remote(
+            flat_ref.at[:, last, edge], top_side, send.at[4], recv.at[3], {"az": below, "rg": 1 - rg}
+        ),
+    ]
+    signal(partner)
+
+    @pl.when(az > 0)
+    def _():
+        signal({"az": above, "rg": rg})
+        signal({"az": above, "rg": 1 - rg})
+
+    @pl.when(az < count_az - 1)
+    def _():
+        signal({"az": below, "rg": rg})
+        signal({"az": below, "rg": 1 - rg})
+
+    has_above = (az > 0).astype(jnp.int32)
+    has_below = (az < count_az - 1).astype(jnp.int32)
+    pl.semaphore_wait(barrier, 1 + 2 * has_above + 2 * has_below)
+
+    @pl.when(az > 0)
+    def _():
+        for copy in up:
+            copy.start()
+
+    @pl.when(az < count_az - 1)
+    def _():
+        for copy in down:
+            copy.start()
+
+    side_copy.start()
+
+    def place(rows, centre, beside):
+        left = jnp.where(rg == 1, beside, 0.0)
+        right = jnp.where(rg == 0, beside, 0.0)
+        for part in range(2):
+            wide = jnp.concatenate([left[part], centre[part], right[part]], axis=1)
+            padded_ref[part, rows, :] = wide[:, LANES - rim : 2 * LANES - rim + samples]
+
+    side_copy.wait()
+    place(slice(rim, rim + lines), flat_ref[...], side[...])
+
+    @pl.when(az > 0)
+    def _():
+        for copy in up:
+            copy.wait_send()
+
+    @pl.when(az < count_az - 1)
+    def _():
+        for copy in down:
+            copy.wait_send()
+
+    @pl.when(az > 0)
+    def _():
+        for copy in down:
+            copy.wait_recv()
+        place(slice(0, rim), top[...], top_side[...])
+
+    @pl.when(az == 0)
+    def _():
+        padded_ref[:, :rim, :] = jnp.zeros((2, rim, padded_ref.shape[2]), F32)
+
+    @pl.when(az < count_az - 1)
+    def _():
+        for copy in up:
+            copy.wait_recv()
+        place(slice(rim + lines, 2 * rim + lines), bottom[...], bottom_side[...])
+
+    @pl.when(az == count_az - 1)
+    def _():
+        padded_ref[:, rim + lines :, :] = jnp.zeros((2, rim, padded_ref.shape[2]), F32)
+
+
+def reduce_kernel(count_az, sums_ref, out_ref, half, near, far, near_send, near_recv, far_send, far_recv):
+    channels, rows, lanes = half.shape
+    tile = rows // count_az
+    az, rg, others, partner = peers(count_az)
+    greet(others + [partner])
+    mine = pl.ds(pl.multiple_of(rg * lanes, LANES), lanes)
+    theirs = pl.ds(pl.multiple_of((1 - rg) * lanes, LANES), lanes)
+    near_copies = [
+        remote(sums_ref.at[c, :, theirs], near.at[c], near_send.at[c], near_recv.at[c], partner)
+        for c in range(channels)
+    ]
+    for copy in near_copies:
+        copy.start()
+    for c, copy in enumerate(near_copies):
+        copy.wait()
+        half[c] = sums_ref[c, :, mine] + near[c]
+    copies = []
+    for d, device in enumerate(others):
+        start = pl.multiple_of(device["az"] * tile, 8)
+        copy = remote(
+            half.at[:, pl.ds(start, tile), :], far.at[d], far_send.at[d], far_recv.at[d], device
+        )
+        copy.start()
+        copies.append(copy)
+    total = half[:, pl.ds(pl.multiple_of(az * tile, 8), tile), :]
+    for d, copy in enumerate(copies):
+        copy.wait()
+        total = total + far[d]
+    out_ref[...] = total[:2] / jnp.maximum(total[2:3], 1.0)
+
+
 def body(
     complex_phase_image,
     phase_to_topography_factor,
@@ -280,41 +454,60 @@
 ):
     count_az = lax.axis_size("az")
     count_rg = lax.axis_size("rg")
-    self_az = lax.axis_index("az")
-    self_rg = lax.axis_index("rg")
-    parcel_north_coordinate, parcel_east_coordinate, number_terrain_points = (
-        terrain_model_heights.shape
-    )
-    nlon_count = parcel_east_coordinate * count_rg
-    own_list = radar_parcel_listing[0]
-    lat_own, lon_own = block_coords(own_list, nlon_count)
-    all_lists = lax.all_gather(radar_parcel_listing, ("az", "rg"), axis=0, tiled=True)
-    lat_all, lon_all = block_coords(all_lists, nlon_count)
-    key_all = lat_all // parcel_north_coordinate * count_rg + lon_all // parcel_east_coordinate
-    local_all = (lat_all - self_az * parcel_north_coordinate) * parcel_east_coordinate + (
-        lon_all - self_rg * parcel_east_coordinate
-    )
-    outgoing = pack_blocks(
-        all_lists,
-        key_all,
-        local_all,
-        terrain_model_heights.reshape(
-            parcel_north_coordinate * parcel_east_coordinate, number_terrain_points
-        ),
-        self_az * count_rg + self_rg,
-    )
-    received = lax.all_to_all(outgoing, ("az", "rg"), split_axis=0, concat_axis=0, tiled=True)
-    key_own = lat_own // parcel_north_coordinate * count_rg + lon_own // parcel_east_coordinate
-    height_lookup_table = unpack_blocks(own_list, key_own, received)
+    assert count_rg == 2
+    north, east, points = terrain_model_heights.shape
+    slots = radar_parcel_listing.shape[1]
     az_lines, rg_samples = phase_to_topography_factor.shape
+    dma = pltpu.SemaphoreType.DMA
+    block = (points // LANES, LANES)
+    listing = jnp.broadcast_to(jnp.pad(radar_parcel_listing, ((0, 0), (0, LANES - slots))), (8, LANES))
+    table = pl.pallas_call(
+        functools.partial(terrain_kernel, count_az, (north, east)),
+        out_shape=jax.ShapeDtypeStruct((slots,) + block, F32),
+        scratch_shapes=[
+            pltpu.VMEM((north * east + north + 1,) + block, F32),
+            pltpu.VMEM((north,) + block, F32),
+            pltpu.VMEM((count_az, 8, LANES), jnp.int32),
+            pltpu.SMEM((count_az, 8, LANES), jnp.int32),
+            pltpu.VMEM((count_az - 1, slots) + block, F32),
+            pltpu.VMEM((count_az - 1, slots) + block, F32),
+            dma((2,)),
+            dma((count_az - 1,)),
+            dma((count_az - 1,)),
+            dma((count_az - 1,)),
+            dma((count_az - 1,)),
+            dma,
+        ],
+        compiler_params=pltpu.CompilerParams(collective_id=0, has_side_effects=True),
+        name="terrain",
+    )(listing, terrain_model_heights.reshape((north * east,) + block))
     flattened = pl.pallas_call(
         flatten_tile,
         out_shape=jax.ShapeDtypeStruct((2, az_lines, rg_samples), F32),
         name="flatten",
-    )(complex_phase_image, phase_to_topography_factor, pixel_terrain_position, height_lookup_table)
+    )(
+        complex_phase_image,
+        phase_to_topography_factor,
+        pixel_terrain_position,
+        table.reshape(-1, LANES),
+    )
     rim = PATCH // 4
-    padded = padded_2(flattened, (("az", 1), ("rg", 2)), rim)
-    padded = jnp.pad(padded, ((0, 0), (0, 0), (0, LANES - 2 * rim)))
+    padded = pl.pallas_call(
+        functools.partial(halo_kernel, count_az, rim),
+        out_shape=jax.ShapeDtypeStruct((2, az_lines + 2 * rim, rg_samples + LANES), F32),
+        in_specs=[pl.BlockSpec(memory_space=pltpu.VMEM)],
+        scratch_shapes=[
+            pltpu.VMEM((2, rim, rg_samples), F32),
+            pltpu.VMEM((2, rim, rg_samples), F32),
+            pltpu.VMEM((2, az_lines, LANES), F32),
+            pltpu.VMEM((2, rim, LANES), F32),
+            pltpu.VMEM((2, rim, LANES), F32),
+            dma((5,)),
+            dma((5,)),
+        ],
+        compiler_params=pltpu.CompilerParams(collective_id=1, has_side_effects=True),
+        name="halo",
+    )(flattened)
     map_lat = az_lines // LOOK
     map_lon = rg_samples // LOOK
     chunks = map_lat * map_lon // LANES
@@ -335,9 +528,24 @@
         multilook_splat_shares.reshape(4, chunks, LANES),
         *tables,
     )
-    sums = lax.psum_scatter(sums, "rg", scatter_dimension=2, tiled=True)
-    sums = lax.psum_scatter(sums, "az", scatter_dimension=1, tiled=True)
-    return sums[:2] / jnp.maximum(sums[2:3], 1.0)
+    return pl.pallas_call(
+        functools.partial(reduce_kernel, count_az),
+        out_shape=jax.ShapeDtypeStruct((2, map_lat, map_lon), F32),
+        in_specs=[pl.BlockSpec(memory_space=pltpu.VMEM)],
+        scratch_shapes=[
+            pltpu.VMEM((3, map_lat * count_az, map_lon), F32),
+            pltpu.VMEM((3, map_lat * count_az, map_lon), F32),
+            pltpu.VMEM((count_az - 1, 3, map_lat, map_lon), F32),
+            dma((3,)),
+            dma((3,)),
+            dma((count_az - 1,)),
+            dma((count_az - 1,)),
+        ],
+        compiler_params=pltpu.CompilerParams(
+            collective_id=2, has_side_effects=True, vmem_limit_bytes=48 * 1024 * 1024
+        ),
+        name="reduce",
+    )(sums)
 
 
 def solution(mesh):

time: 181 us -> 59.4 us (0.33)
  waiting for transfers between devices: 105 us -> 0 us
  Pallas kernels: 17.6 us -> 53.5 us
  blocking collectives: 23 us -> 0 us
  between operations: 13.8 us -> 0.19 us
  starting transfers between devices: 12.1 us -> 0 us
  other arithmetic: 4.42 us -> 0 us
    reduce_scatter x2 -> x0, waiting for transfers between devices: 74.3 us -> none  [the longest x1 66 us: body(): sums = lax.psum_scatter(sums, 'az', scatter_dimension=1, tiled=True)]
    pallas_call x0 -> x3, Pallas kernels: none -> 36.7 us  [the longest x1 20.8 us: body(): pl.pallas_call(functools.partial(terrain_kernel, count_az, (north, east))...]
    all_gather x1 -> x0, blocking collectives: 23 us -> none  [body(): lax.all_gather(radar_parcel_listing, ('az', 'rg'), axis=0, tiled=True)]
    all_to_all x1 -> x0, waiting for transfers between devices: 22.5 us -> none  [body(): lax.all_to_all(outgoing, ('az', 'rg'), split_axis=0, concat_axis=0, tiled...]
    ppermute x4 -> x0, starting transfers between devices: 8.41 us -> none  [the longest x2 5.64 us: padded_2(): before = lax.ppermute(last, axis, up)]
    ppermute x4 -> x0, waiting for transfers between devices: 7.85 us -> none  [the longest x2 6.89 us: padded_2(): after = lax.ppermute(first, axis, down)]
    all_to_all x1 -> x0, starting transfers between devices: 3.65 us -> none  [body(): lax.all_to_all(outgoing, ('az', 'rg'), split_axis=0, concat_axis=0, tiled...]
    unnamed x33 -> x31, local copies, waits for them, and re-layouts: 1.35 us -> 4.8 us
  transfers between devices with their start and end apart: 7 -> 0, of which waited for: 6 -> 0; matrix products, arithmetic and copies ran while one was open for 0% -> 0% of each run, Pallas kernels for 0% -> 0%
where the time goes in v2:
time: 59.4 us; the launch traced here: 59.1 us
  Pallas kernels  53.5 us (90%)
  local copies, waits for them, and re-layouts  5.4 us (9%)
    pallas_call x1, Pallas kernels, body(): pl.pallas_call(functools.partial(terrain_kernel, count_az, (north, east))...  20.8 us
    pallas_call x1, Pallas kernels, body(): pl.pallas_call(functools.partial(reduce_kernel, count_az), out_shape=jax....  9.29 us
    pallas_call x1, Pallas kernels, body(): pl.pallas_call(functools.partial(filter_kernel, (map_lat, map_lon)), out_...  8.44 us
    pallas_call x1, Pallas kernels, body(): pl.pallas_call(flatten_tile, out_shape=jax.ShapeDtypeStruct((2, az_lines,...  8.42 us
    pallas_call x1, Pallas kernels, body(): pl.pallas_call(functools.partial(halo_kernel, count_az, rim), out_shape=j...  6.59 us
    unnamed x31, local copies, waits for them, and re-layouts  4.8 us

profile of v2, /device:TPU:0, one launch (start us, length us, event | category | flops | bytes accessed | tf_op | source)
XLA Modules:
  0.0 59.1 jit_solution(16352522501558535566)
XLA Ops:
  0.0 0.7 %copy-done.13 = s32[1,9]{1,0:T(1,128)S(1)} copy-done((s32[1,9]{1,0:T(1,128)S(1)}, s32[1,9]{1,0:T(1,128)}, u32[]{:S(2)}) %copy-start.13) | copy-done | bytes 60
  0.7 0.6 %broadcast_in_dim.8.list_ref = s32[8,128]{1,0:T(8,128)} broadcast(s32[128]{0:T(128)S(1)} %pad_bitcast_fusion), dimensions={1} | broadcast | bytes 4608 | tf_op jit(solution)/shard_map/broadcast_in_dim | solution.py:463
  1.3 0.8 %copy.22 = f32[1,4,16,128]{3,2,1,0:T(8,128)S(1)} copy(f32[1,4,16,128]{3,1,2,0:T(4,128)} %bitcast.18) | data formatting | bytes 65536
  2.0 1.7 %copy.19 = f32[8,8,8,128]{3,2,1,0:T(8,128)} copy(f32[8,8,8,128]{3,1,2,0:T(8,128)} %bitcast.16) | data formatting | bytes 524288
  3.7 0.0 copy-start.12
  3.7 20.8 %terrain.1 = f32[9,8,128]{2,1,0:T(8,128)} custom-call(s32[8,128]{1,0:T(8,128)} %broadcast_in_dim.8.list_ref, f32[64,8,128]{2,1,0:T(8,128)} %bitcast.15), custom_call_target="tpu_custom_call" | custom-call | tf_op jit(solution)/shard_map/terrain/pallas_call | solution.py:464
  24.5 0.0 copy-start.2
  24.5 0.0 copy-start.4
  24.5 0.0 copy-start.5
  24.6 0.0 copy-start.6
  24.6 8.4 %flatten.1.flat_ref = f32[2,64,512]{2,1,0:T(8,128)} custom-call(f32[2,64,512]{2,1,0:T(8,128)} %image_ref.1, f32[64,512]{1,0:T(8,128)} %factor_ref.1, s32[64,512]{1,0:T(8,128)} %position_ref.1, f32[72,128]{1,0:T(8,128)} %bitcast.17), custom_call_target="tpu_custom_call" | custom-call | tf_op jit(solution)/shard_map/flatten/pallas_call | solution.py:484
  33.0 6.6 %halo.1.padded_ref = f32[2,96,640]{2,1,0:T(8,128)} custom-call(f32[2,64,512]{2,1,0:T(8,128)} %flatten.1.flat_ref), custom_call_target="tpu_custom_call" | custom-call | tf_op jit(solution)/shard_map/halo/pallas_call | solution.py:495
  39.6 0.0 copy-done.7
  39.6 0.0 copy-done.8
  39.6 0.0 copy-done.9
  39.6 0.0 copy-done.10
  39.6 0.0 copy-done.12
  39.6 0.0 copy-done.2
  39.6 0.0 copy-done.4
  39.7 0.0 copy-done.5
  39.7 1.0 %copy-done = f32[2,96,640]{2,1,0:T(8,128)S(1)} copy-done((f32[2,96,640]{2,1,0:T(8,128)S(1)}, f32[2,96,640]{2,1,0:T(8,128)}, u32[]{:S(2)}) %copy-start) | copy-done | bytes 491544
  40.7 8.4 %filter_splat.1.sums_ref = f32[3,128,256]{2,1,0:T(8,128)S(1)} custom-call(f32[2,96,640]{2,1,0:T(8,128)S(1)} %copy-done, s32[16,128]{1,0:T(8,128)S(1)} %bitcast.13, s32[16,128]{1,0:T(8,128)S(1)} %bitcast.14, f32[4,16,128]{2,1,0:T(8,128)S(1)} %bitcast.12, bf16[128,128]{1,0:T(8,128)(2,1)S(1)} %copy-done.8, bf16[128,128]{1,0:T(8,128)(2,1)S(1)} %copy-done.7, ...), custom_call_target="tpu_custom_call" | custom-call | tf_op jit(solution)/shard_map/filter_splat/pallas_call | solution.py:515
  49.2 9.3 %reduce.1 = f32[2,16,128]{2,1,0:T(8,128)S(1)} custom-call(f32[3,128,256]{2,1,0:T(8,128)S(1)} %filter_splat.1.sums_ref), custom_call_target="tpu_custom_call" | custom-call | tf_op jit(solution)/shard_map/reduce/pallas_call | solution.py:531
  58.5 0.6 %copy.24 = f32[2,16,128]{2,1,0:T(8,128)} copy(f32[2,16,128]{2,1,0:T(8,128)S(1)} %reduce.1) | data formatting | bytes 32768
  (14 shorter events, 0.0 us)
Async XLA Ops:
  0.0 0.7 %copy-start.13 = (s32[1,9]{1,0:T(1,128)S(1)}, s32[1,9]{1,0:T(1,128)}, u32[]{:S(2)}) copy-start(s32[1,9]{1,0:T(1,128)} %param.21) | copy-start | bytes 112
  3.7 35.9 %copy-start.7 = (bf16[128,128]{1,0:T(8,128)(2,1)S(1)}, bf16[128,128]{1,0:T(8,128)(2,1)}, u32[]{:S(2)}) copy-start(bf16[128,128]{1,0:T(8,128)(2,1)} %constant.23.clone.refs_1_) | copy-start | bytes 98308
  3.7 35.9 %copy-start.8 = (bf16[128,128]{1,0:T(8,128)(2,1)S(1)}, bf16[128,128]{1,0:T(8,128)(2,1)}, u32[]{:S(2)}) copy-start(bf16[128,128]{1,0:T(8,128)(2,1)} %constant.22.clone.refs_0_) | copy-start | bytes 98308
  3.7 35.9 %copy-start.9 = (s32[2048,1]{0,1:T(1,128)S(1)}, s32[2048,1]{0,1:T(1,128)}, u32[]{:S(2)}) copy-start(s32[2048,1]{0,1:T(1,128)} %param.23) | copy-start | bytes 24580
  3.7 35.9 %copy-start.10 = (s32[2048]{0:T(1024)S(1)}, s32[2048]{0:T(1024)}, u32[]{:S(2)}) copy-start(s32[2048]{0:T(1024)} %param.24) | copy-start | bytes 24580
  3.7 35.9 %copy-start.12 = (bf16[16,128]{1,0:T(8,128)(2,1)S(1)}, bf16[16,128]{1,0:T(8,128)(2,1)}, u32[]{:S(2)}) copy-start(bf16[16,128]{1,0:T(8,128)(2,1)} %constant.26.clone.refs_4_) | copy-start | bytes 12292
  24.5 15.1 %copy-start.2 = (bf16[512,512]{1,0:T(8,128)(2,1)S(1)}, bf16[512,512]{1,0:T(8,128)(2,1)}, u32[]{:S(2)}) copy-start(bf16[512,512]{1,0:T(8,128)(2,1)} %constant.24.clone.refs_2_) | copy-start | bytes 1572868
  24.5 15.1 %copy-start.4 = (bf16[256,256]{1,0:T(8,128)(2,1)S(1)}, bf16[256,256]{1,0:T(8,128)(2,1)}, u32[]{:S(2)}) copy-start(bf16[256,256]{1,0:T(8,128)(2,1)} %constant.30.clone.refs_8_) | copy-start | bytes 393220
  24.5 15.1 %copy-start.5 = (bf16[512,64]{1,0:T(8,128)(2,1)S(1)}, bf16[512,64]{1,0:T(8,128)(2,1)}, u32[]{:S(2)}) copy-start(bf16[512,64]{1,0:T(8,128)(2,1)} %constant.29.clone.refs_7_) | copy-start | bytes 196612
  24.6 15.1 %copy-start.6 = (bf16[512,64]{1,0:T(8,128)(2,1)S(1)}, bf16[512,64]{1,0:T(8,128)(2,1)}, u32[]{:S(2)}) copy-start(bf16[512,64]{1,0:T(8,128)(2,1)} %constant.28.clone.refs_6_) | copy-start | bytes 196612
  33.0 6.7 %copy-start.1 = (bf16[512,512]{1,0:T(8,128)(2,1)S(1)}, bf16[512,512]{1,0:T(8,128)(2,1)}, u32[]{:S(2)}) copy-start(bf16[512,512]{1,0:T(8,128)(2,1)} %constant.25.clone.refs_3_) | copy-start | bytes 1572868
  33.0 6.7 %copy-start.3 = (bf16[256,256]{1,0:T(8,128)(2,1)S(1)}, bf16[256,256]{1,0:T(8,128)(2,1)}, u32[]{:S(2)}) copy-start(bf16[256,256]{1,0:T(8,128)(2,1)} %constant.31.clone.refs_9_) | copy-start | bytes 393220
  33.0 6.7 %copy-start.11 = (bf16[16,128]{1,0:T(8,128)(2,1)S(1)}, bf16[16,128]{1,0:T(8,128)(2,1)}, u32[]{:S(2)}) copy-start(bf16[16,128]{1,0:T(8,128)(2,1)} %constant.27.clone.refs_5_) | copy-start | bytes 12292
  39.7 1.0 %copy-start = (f32[2,96,640]{2,1,0:T(8,128)S(1)}, f32[2,96,640]{2,1,0:T(8,128)}, u32[]{:S(2)}) copy-start(f32[2,96,640]{2,1,0:T(8,128)} %halo.1.padded_ref) | copy-start | bytes 1474564
